TPU v7x, 32 devices: a whole 2x2x4 slice. The times are simulated.
32 devices in a mesh: dp: 4 (over x, core), expert: 8 (over z, y).
Axes of the slice: x: 2, y: 2, z: 4, core: 2. Of those that a mesh axis runs over, the one named last changes fastest.
Arguments:
- tokens: bfloat16 [4, 1024, 2048], P('dp', 'expert'), may hold values from -6 to 6
- cotangent: bfloat16 [4, 1024, 2048], P('dp', 'expert'), may hold values from -0.796875 to 0.796875
- w_gate: bfloat16 [8, 2048, 384], P('expert'), may hold values from -0.125 to 0.125
- w_up: bfloat16 [8, 2048, 384], P('expert'), may hold values from -0.125 to 0.125
- w_down: bfloat16 [8, 384, 2048], P('expert'), may hold values from -0.3125 to 0.3125
- route_owner: int32 [4, 8, 256], P('dp'), may hold values from 0 to 7, as said below
- route_row: int32 [4, 8, 256], P('dp'), may hold values from 0 to 127
- gates: float32 [4, 8, 256], P('dp', 'expert'), may hold values from 0.1 to 1
Outputs:
- token_grads: bfloat16 [4, 1024, 2048], P('dp', 'expert')
- grad_gate: float32 [8, 2048, 384], P('expert', 'dp')
- grad_up: float32 [8, 2048, 384], P('expert', 'dp')
- grad_down: float32 [8, 384, 2048], P('expert', None, 'dp')
- gate_grads: float32 [4, 8, 256], P('dp', 'expert')
Inputs may be any that keep to these rules, and one draw needn't show every extreme that they name: Within one group and expert no (route_owner, route_row) pair repeats; an expert takes at most 40 tokens of one device, and exactly 40 of at least one device.
All inputs are finite; a program needn't handle non-finite values.
Results may differ from a plain program's by a relative error of at most 0.008.
Values may be sent and summed in bfloat16 or wider, within the bound.
A program may use at most 64 MiB of HBM per device.

v0:
```python
import functools

import jax
import jax.numpy as jnp
from jax import lax
from jax.experimental import pallas as pl
from jax.experimental.pallas import tpu as pltpu
from jax.sharding import PartitionSpec as P


def contract_first(left, right):
    return lax.dot_general(
        left, right, (((0,), (0,)), ((), ())), preferred_element_type=jnp.float32
    )


def contract_last(left, right):
    return lax.dot_general(
        left, right, (((1,), (1,)), ((), ())), preferred_element_type=jnp.float32
    )


def on_device(tokens, cotangent, w_gate, w_up, w_down, route_owner, route_row, gates):
    peers = lax.axis_size("expert")
    device = lax.axis_index("expert")
    local_tokens = tokens[0]
    local_cotangent = cotangent[0]
    gate_matrix = w_gate[0]
    up_matrix = w_up[0]
    down_matrix = w_down[0]
    owners_all = route_owner[0]
    rows_all = route_row[0]
    token_count = local_tokens.shape[0]
    width = local_tokens.shape[1]
    slots_each = owners_all.shape[1]
    capacity = (5 * slots_each + 4 * peers - 1) // (4 * peers)
    held_here = owners_all == device
    ranks_here = jnp.cumsum(held_here.astype(jnp.int32), axis=1) - 1
    levels = jnp.arange(capacity, dtype=jnp.int32)
    matches = held_here[None, :, :] & (ranks_here[None, :, :] == levels[:, None, None])
    wanted_by_level = jnp.sum(jnp.where(matches, rows_all[None, :, :] + 1, 0), axis=2) - 1
    wanted = wanted_by_level.T.reshape(-1)
    selector = (wanted[:, None] == jnp.arange(token_count, dtype=jnp.int32)[None, :]).astype(
        jnp.bfloat16
    )
    send_inputs = jnp.dot(selector, local_tokens, preferred_element_type=jnp.float32).astype(
        jnp.bfloat16
    )
    send_outputs = jnp.dot(selector, local_cotangent, preferred_element_type=jnp.float32).astype(
        jnp.bfloat16
    )
    got_inputs = lax.all_to_all(
        send_inputs.reshape(peers, capacity * width),
        "expert",
        split_axis=0,
        concat_axis=0,
        tiled=True,
    )
    got_outputs = lax.all_to_all(
        send_outputs.reshape(peers, capacity * width),
        "expert",
        split_axis=0,
        concat_axis=0,
        tiled=True,
    )
    own_owner = lax.dynamic_index_in_dim(owners_all, device, 0, keepdims=False)
    own_gate = gates[0, 0]
    owner_hits = (own_owner[:, None] == jnp.arange(peers, dtype=jnp.int32)[None, :]).astype(
        jnp.int32
    )
    own_rank = jnp.sum(owner_hits * (jnp.cumsum(owner_hits, axis=0) - 1), axis=1)
    slot_index = own_owner * capacity + own_rank
    flat_inputs = got_inputs.reshape(peers * capacity, width)
    flat_outputs = got_outputs.reshape(peers * capacity, width)
    rows_in = jnp.take(flat_inputs, slot_index, axis=0)
    rows_out = jnp.take(flat_outputs, slot_index, axis=0)
    pre_gate = jnp.dot(rows_in, gate_matrix, preferred_element_type=jnp.float32)
    pre_up = jnp.dot(rows_in, up_matrix, preferred_element_type=jnp.float32)
    sigma = jax.nn.sigmoid(pre_gate)
    activated = pre_gate * sigma
    hidden = (activated * pre_up).astype(jnp.bfloat16)
    expert_out = jnp.dot(hidden, down_matrix, preferred_element_type=jnp.float32)
    gate_grad_rows = jnp.sum(rows_out.astype(jnp.float32) * expert_out, axis=1)
    scaled = (own_gate[:, None] * rows_out.astype(jnp.float32)).astype(jnp.bfloat16)
    d_hidden = contract_last(scaled, down_matrix)
    d_pre_gate = (d_hidden * pre_up * sigma * (1.0 + pre_gate * (1.0 - sigma))).astype(jnp.bfloat16)
    d_pre_up = (d_hidden * activated).astype(jnp.bfloat16)
    row_grad = (contract_last(d_pre_gate, gate_matrix) + contract_last(d_pre_up, up_matrix)).astype(
        jnp.bfloat16
    )
    gate_part = contract_first(rows_in, d_pre_gate)
    up_part = contract_first(rows_in, d_pre_up)
    down_part = contract_first(scaled, hidden)
    gate_sum, up_sum, down_sum = (
        lax.psum_scatter(
            gate_part.astype(jnp.bfloat16), "dp", scatter_dimension=0, tiled=True
        ).astype(jnp.float32),
        lax.psum_scatter(
            up_part.astype(jnp.bfloat16), "dp", scatter_dimension=0, tiled=True
        ).astype(jnp.float32),
        lax.psum_scatter(
            down_part.astype(jnp.bfloat16), "dp", scatter_dimension=0, tiled=True
        ).astype(jnp.float32),
    )
    back_rows = jnp.zeros((peers * capacity, width), jnp.bfloat16).at[slot_index].set(row_grad)
    got_back = lax.all_to_all(
        back_rows.reshape(peers, capacity * width),
        "expert",
        split_axis=0,
        concat_axis=0,
        tiled=True,
    )
    token_grads = contract_first(selector, got_back.reshape(peers * capacity, width)).astype(
        jnp.bfloat16
    )
    return (
        token_grads[None],
        gate_sum[None],
        up_sum[None],
        down_sum.T[None],
        gate_grad_rows[None, None],
    )


MESH = pl.DeviceIdType.MESH
F32 = jnp.float32
BF16 = jnp.bfloat16
ORDER = (6, 7, 4, 5, 2, 3, 1)


def flipped(index, bits, size):
    out = 0
    step = 1
    while step < size:
        out = out + step * (((index // step) % 2 + (bits // step) % 2) % 2)
        step *= 2
    return out


def dot(left, right):
    return jnp.dot(left, right, preferred_element_type=F32)


def fused(
    peers, cap, tok_hbm, cot_hbm, wg_hbm, wu_hbm, wd_hbm, owner_ref, row_ref, gates_ref,
    tg_out, gg_out, gu_out, gd_out, gr_out,
    tt, cc, wgu, wd, code_ref, sel, put, take, send, got, back_send, back_got,
    rows, pre, dpre, hid, outg,
    core_send_a, core_got_a, own_a, x_send_a, x_got_a,
    core_send_b, core_got_b, own_b, x_send_b, x_got_b,
    load_sem, send_sem, recv_sem, bsend_sem, brecv_sem, csend_sem, crecv_sem, xsend_sem, xrecv_sem,
):
    me = lax.axis_index("expert")
    dp = lax.axis_index("dp")
    plane, core = dp // 2, dp % 2
    sibling = plane * 2 + (1 - core)
    across = (1 - plane) * 2 + core
    tokens_here, width = tok_hbm.shape
    half = width // 2
    slots = owner_ref.shape[1]
    ff = wg_hbm.shape[1]
    shard = width // 4
    slab = 2 * cap
    partners = {k: flipped(me, k, peers) for k in range(peers)}

    loads = []
    for number, (src, dst) in enumerate((
        (tok_hbm.at[:, pl.ds(0, half)], tt.at[pl.ds(0, tokens_here)]),
        (tok_hbm.at[:, pl.ds(half, half)], tt.at[pl.ds(tokens_here, tokens_here)]),
        (cot_hbm.at[:, pl.ds(0, half)], cc.at[pl.ds(0, tokens_here)]),
        (cot_hbm.at[:, pl.ds(half, half)], cc.at[pl.ds(tokens_here, tokens_here)]),
        (wg_hbm, wgu.at[:, pl.ds(0, ff)]),
        (wu_hbm, wgu.at[:, pl.ds(ff, ff)]),
        (wd_hbm, wd),
    )):
        copy = pltpu.make_async_copy(src, dst, load_sem.at[number])
        copy.start()
        loads.append(copy)

    barrier = pltpu.get_barrier_semaphore()
    for k in ORDER:
        pl.semaphore_signal(barrier, inc=1, device_id=(dp, partners[k]), device_id_type=MESH)
    for other in (sibling, across):
        pl.semaphore_signal(barrier, inc=1, device_id=(other, me), device_id_type=MESH)

    before = (
        lax.broadcasted_iota(jnp.int32, (slots, slots), 0)
        < lax.broadcasted_iota(jnp.int32, (slots, slots), 1)
    ).astype(F32).astype(BF16)
    held = owner_ref[...] == me
    code_ref[...] = jnp.where(held, dot(held.astype(F32).astype(BF16), before), -1.0)
    line = lax.broadcasted_iota(jnp.int32, (slab, 1), 0)
    level = jnp.where(line < cap, line, line - cap).astype(F32)
    first = line < cap
    spots = lax.broadcasted_iota(jnp.int32, (tokens_here, 1), 0)
    for k in ORDER + (0,):
        wanted = code_ref[pl.ds(partners[k], 1), :]
        at_level = (wanted == level).astype(F32).astype(BF16)
        at_row = (row_ref[pl.ds(partners[k], 1), :] == spots).astype(F32).astype(BF16)
        chosen = contract_last(at_level, at_row)
        sel[pl.ds(k * slab, slab), pl.ds(0, tokens_here)] = jnp.where(first, chosen, 0.0).astype(BF16)
        sel[pl.ds(k * slab, slab), pl.ds(tokens_here, tokens_here)] = jnp.where(
            first, 0.0, chosen
        ).astype(BF16)

    pl.semaphore_wait(barrier, peers - 1 + 2)

    copies = []
    forward = {}
    for which, table in ((0, tt), (1, cc)):
        loads[2 * which].wait()
        loads[2 * which + 1].wait()
        for k in ORDER + (0,):
            for piece in range(0, half, 512):
                picked = dot(
                    sel[pl.ds(k * slab, slab), :], table[:, pl.ds(piece, 512)]
                ).astype(BF16)
                if k:
                    send[which, k, :, pl.ds(piece, 512)] = picked
                else:
                    got[which, k, :, pl.ds(piece, 512)] = picked
            if k:
                copy = pltpu.make_async_remote_copy(
                    src_ref=send.at[which, k],
                    dst_ref=got.at[which, k],
                    send_sem=send_sem.at[which, k],
                    recv_sem=recv_sem.at[which, k],
                    device_id=(dp, partners[k]),
                    device_id_type=MESH,
                )
                copy.start()
                copies.append(copy)
                forward[which, k] = copy

    own_owner = owner_ref[pl.ds(me, 1), :]
    owned = own_owner == lax.broadcasted_iota(jnp.int32, (peers, 1), 0)
    ranks = dot(owned.astype(F32).astype(BF16), before)
    own_rank = jnp.sum(jnp.where(owned, ranks, 0.0), axis=0, keepdims=True)
    for k in range(peers):
        hit = ((own_owner == partners[k]) & (own_rank == level)).astype(F32)
        left, right = jnp.where(first, hit, 0.0), jnp.where(first, 0.0, hit)
        put[pl.ds(k * slab, slab), pl.ds(0, slots)] = left.astype(BF16)
        put[pl.ds(k * slab, slab), pl.ds(slots, slots)] = right.astype(BF16)
    for part in range(0, peers * slab, 128):
        take[:, pl.ds(part, 128)] = put[pl.ds(part, 128), :].astype(F32).T.astype(BF16)
    weight = jnp.broadcast_to(gates_ref[...], (128, slots)).T[:, :1]
    for number in (4, 5, 6):
        loads[number].wait()

    def pick(which):
        for k in ORDER:
            forward[which, k].wait_recv()
        flat = got.at[which].reshape(peers * slab, half)

        for piece in range(0, half, 256):
            picked = dot(take[...], flat[:, pl.ds(piece, 256)]).astype(BF16)
            rows[which, :, pl.ds(piece, 256)] = picked[:slots]
            rows[which, :, pl.ds(half + piece, 256)] = picked[slots:]

    pick(0)
    pre[...] = dot(rows[0], wgu[...])
    pick(1)
    raw = contract_last(rows[1], wd[...])
    pre_gate = pre[:, :ff]
    pre_up = pre[:, ff:]
    sigma = jax.nn.sigmoid(pre_gate)
    activated = pre_gate * sigma
    hidden = activated * pre_up
    gate_rows = jnp.sum(hidden * raw, axis=1, keepdims=True)
    gr_out[...] = jnp.broadcast_to(gate_rows, (slots, 128)).T[:1]
    hid[...] = (hidden * weight).astype(BF16)
    d_hidden = raw * weight
    dpre[:, :ff] = (d_hidden * pre_up * sigma * (1.0 + pre_gate * (1.0 - sigma))).astype(BF16)
    dpre[:, ff:] = (d_hidden * activated).astype(BF16)

    for piece in range(0, half, 512):
        for side in range(2):
            grad = contract_last(dpre[...], wgu[pl.ds(side * half + piece, 512), :])
            outg[pl.ds(side * slots, slots), pl.ds(piece, 512)] = grad.astype(BF16)
    backward = {}
    for k in ORDER + (0,):
        for piece in range(0, half, 512):
            placed = dot(
                put[pl.ds(k * slab, slab), :], outg[:, pl.ds(piece, 512)]
            ).astype(BF16)
            if k:
                back_send[k, :, pl.ds(piece, 512)] = placed
            else:
                back_got[k, :, pl.ds(piece, 512)] = placed
        if k:
            copy = pltpu.make_async_remote_copy(
                src_ref=back_send.at[k],
                dst_ref=back_got.at[k],
                send_sem=bsend_sem.at[k],
                recv_sem=brecv_sem.at[k],
                device_id=(dp, partners[k]),
                device_id_type=MESH,
            )
            copy.start()
            copies.append(copy)
            backward[k] = copy

    def parts(owner):
        columns = pl.ds(pl.multiple_of(owner * shard, shard), shard)
        return (
            contract_first(rows[0, :, columns], dpre[...]),
            contract_first(hid[...], rows[1, :, columns]),
        )

    planes = (1 - plane, plane)
    core_copies = {}
    for j in range(2):
        one, two = parts(planes[j] * 2 + (1 - core))
        core_send_a[j] = one.astype(BF16)
        core_send_b[j] = two.astype(BF16)
        for n, (src, dst) in enumerate(((core_send_a, core_got_a), (core_send_b, core_got_b))):
            copy = pltpu.make_async_remote_copy(
                src_ref=src.at[j],
                dst_ref=dst.at[j],
                send_sem=csend_sem.at[j, n],
                recv_sem=crecv_sem.at[j, n],
                device_id=(sibling, me),
                device_id_type=MESH,
            )
            copy.start()
            copies.append(copy)
            core_copies[j, n] = copy
        one, two = parts(planes[j] * 2 + core)
        own_a[j] = one
        own_b[j] = two
        if j == 0:
            x_copies = []
            for n, (own, near, src, dst) in enumerate((
                (own_a, core_got_a, x_send_a, x_got_a),
                (own_b, core_got_b, x_send_b, x_got_b),
            )):
                core_copies[0, n].wait_recv()
                src[...] = (own[0] + near[0].astype(F32)).astype(BF16)
                copy = pltpu.make_async_remote_copy(
                    src_ref=src,
                    dst_ref=dst,
                    send_sem=xsend_sem.at[n],
                    recv_sem=xrecv_sem.at[n],
                    device_id=(across, me),
                    device_id_type=MESH,
                )
                copy.start()
                copies.append(copy)
                x_copies.append(copy)
    core_copies[1, 0].wait_recv()
    own_a[1] = own_a[1] + core_got_a[1].astype(F32)
    core_copies[1, 1].wait_recv()
    own_b[1] = own_b[1] + core_got_b[1].astype(F32)

    x_copies[0].wait_recv()
    total = own_a[1] + x_got_a[...].astype(F32)
    gg_out[...] = total[:, :ff]
    gu_out[...] = total[:, ff:]
    x_copies[1].wait_recv()
    gd_out[...] = own_b[1] + x_got_b[...].astype(F32)

    for k in ORDER:
        backward[k].wait_recv()
    flat_back = back_got.reshape(peers * slab, half)
    for piece in range(0, half, 256):
        summed = contract_first(sel[...], flat_back[:, pl.ds(piece, 256)]).astype(BF16)
        tg_out[:, pl.ds(piece, 256)] = summed[:tokens_here]
        tg_out[:, pl.ds(half + piece, 256)] = summed[tokens_here:]
    for copy in copies:
        copy.wait_send()


def by_kernel(cap, tokens, cotangent, w_gate, w_up, w_down, route_owner, route_row, gates):
    peers = route_owner.shape[1]
    slots = route_owner.shape[2]
    tokens_here, width = tokens.shape[1:]
    ff = w_gate.shape[2]
    half, shard, slab = width // 2, width // 4, 2 * cap
    vmem = pl.BlockSpec(memory_space=pltpu.VMEM)
    hbm = pl.BlockSpec(memory_space=pl.ANY)
    dma = pltpu.SemaphoreType.DMA
    outs = pl.pallas_call(
        functools.partial(fused, peers, cap),
        out_shape=(
            jax.ShapeDtypeStruct((tokens_here, width), BF16),
            jax.ShapeDtypeStruct((shard, ff), F32),
            jax.ShapeDtypeStruct((shard, ff), F32),
            jax.ShapeDtypeStruct((ff, shard), F32),
            jax.ShapeDtypeStruct((1, slots), F32),
        ),
        in_specs=[hbm] * 5 + [vmem] * 3,
        out_specs=(vmem,) * 5,
        scratch_shapes=[
            pltpu.VMEM((2 * tokens_here, half), BF16),
            pltpu.VMEM((2 * tokens_here, half), BF16),
            pltpu.VMEM((width, 2 * ff), BF16),
            pltpu.VMEM((ff, width), BF16),
            pltpu.VMEM((peers, slots), F32),
            pltpu.VMEM((peers * slab, 2 * tokens_here), BF16),
            pltpu.VMEM((peers * slab, 2 * slots), BF16),
            pltpu.VMEM((2 * slots, peers * slab), BF16),
            pltpu.VMEM((2, peers, slab, half), BF16),
            pltpu.VMEM((2, peers, slab, half), BF16),
            pltpu.VMEM((peers, slab, half), BF16),
            pltpu.VMEM((peers, slab, half), BF16),
            pltpu.VMEM((2, slots, width), BF16),
            pltpu.VMEM((slots, 2 * ff), F32),
            pltpu.VMEM((slots, 2 * ff), BF16),
            pltpu.VMEM((slots, ff), BF16),
            pltpu.VMEM((2 * slots, half), BF16),
            pltpu.VMEM((2, shard, 2 * ff), BF16),
            pltpu.VMEM((2, shard, 2 * ff), BF16),
            pltpu.VMEM((2, shard, 2 * ff), F32),
            pltpu.VMEM((shard, 2 * ff), BF16),
            pltpu.VMEM((shard, 2 * ff), BF16),
            pltpu.VMEM((2, ff, shard), BF16),
            pltpu.VMEM((2, ff, shard), BF16),
            pltpu.VMEM((2, ff, shard), F32),
            pltpu.VMEM((ff, shard), BF16),
            pltpu.VMEM((ff, shard), BF16),
            dma((7,)),
            dma((2, peers)),
            dma((2, peers)),
            dma((peers,)),
            dma((peers,)),
            dma((2, 2)),
            dma((2, 2)),
            dma((2,)),
            dma((2,)),
        ],
        compiler_params=pltpu.CompilerParams(
            collective_id=0, has_side_effects=True, vmem_limit_bytes=56 * 1024 * 1024
        ),
        name="moe_backward",
    )(
        tokens[0], cotangent[0], w_gate[0], w_up[0], w_down[0],
        route_owner[0], route_row[0], gates[0],
    )
    token_grads, gate_sum, up_sum, down_sum, gate_rows = outs
    return token_grads[None], gate_sum[None], up_sum[None], down_sum[None], gate_rows[None]


def on_device_any(tokens, cotangent, w_gate, w_up, w_down, route_owner, route_row, gates):
    peers = lax.axis_size("expert")
    slots = route_owner.shape[2]
    cap = (5 * slots + 4 * peers - 1) // (4 * peers)
    arrays = (tokens, cotangent, w_gate, w_up, w_down, route_owner, route_row, gates)
    if peers == 8 and lax.axis_size("dp") == 4 and cap % 8 == 0:
        return by_kernel(cap, *arrays)
    return on_device(*arrays)


def solution(mesh):
    return jax.shard_map(
        on_device_any,
        mesh=mesh,
        in_specs=(
            P("dp", "expert", None),
            P("dp", "expert", None),
            P("expert", None, None),
            P("expert", None, None),
            P("expert", None, None),
            P("dp", None, None),
            P("dp", None, None),
            P("dp", "expert", None),
        ),
        out_specs=(
            P("dp", "expert", None),
            P("expert", "dp", None),
            P("expert", "dp", None),
            P("expert", None, "dp"),
            P("dp", "expert", None),
        ),
        check_vma=False,
    )
```

profile of v0, /device:TPU:1, one launch (start us, length us, event | category | flops | bytes accessed | tf_op | source)
XLA Modules:
  0.0 108.3 jit_solution(3343298802430472200)
XLA Ops:
  0.6 101.2 %moe_backward.1 = (bf16[128,2048]{1,0:T(8,128)(2,1)}, f32[512,384]{1,0:T(8,128)}, f32[512,384]{1,0:T(8,128)}, f32[384,512]{1,0:T(8,128)}, f32[1,256]{1,0:T(1,128)}) custom-call(bf16[128,2048]{1,0:T(8,128)(2,1)} %bitcast.19, bf16[128,2048]{1,0:T(8,128)(2,1)} %bitcast.20, bf16[2048,384]{1,0:T(8,128)(2,1)} %bitcast.13, bf16[2048,384]{1,0:T(8,128)(2,1)} %bitcast.14, ...), custom_call_target="tpu_custom_call" | custom-call | tf_op jit(solution)/shard_map/moe_backward/pallas_call | solution.py:382
  101.9 0.0 copy-start.1
  101.9 2.0 %copy.18 = bf16[1,128,2048]{2,1,0:T(8,128)(2,1)} copy(bf16[1,128,2048]{2,1,0:T(8,128)(2,1)} %bitcast.21) | data formatting | bytes 1048576
  103.8 0.0 copy-start
  103.8 2.1 %copy.19 = f32[1,512,384]{2,1,0:T(8,128)} copy(f32[1,512,384]{2,1,0:T(8,128)} %bitcast.18) | data formatting | bytes 1572864
  106.0 0.0 copy-done.1
  106.0 0.0 copy-start.2
  106.0 0.9 copy.20
  106.9 0.0 copy-done
  106.9 0.9 copy.21
  107.8 0.0 copy-done.2
  107.8 0.6 copy.22
Async XLA Ops:
  101.9 4.1 %copy-start.1 = (f32[512,384]{1,0:T(8,128)S(1)}, f32[512,384]{1,0:T(8,128)}, u32[]{:S(2)}) copy-start(f32[512,384]{1,0:T(8,128)} %get-tuple-element.12) | copy-start | bytes 2359300
  103.8 3.0 %copy-start = (f32[384,512]{1,0:T(8,128)S(1)}, f32[384,512]{1,0:T(8,128)}, u32[]{:S(2)}) copy-start(f32[384,512]{1,0:T(8,128)} %get-tuple-element.13) | copy-start | bytes 2359300
  106.0 1.8 %copy-start.2 = (f32[1,256]{1,0:T(1,128)S(1)}, f32[1,256]{1,0:T(1,128)}, u32[]{:S(2)}) copy-start(f32[1,256]{1,0:T(1,128)} %get-tuple-element.14) | copy-start | bytes 3076
where the time goes:
time: 109 us; the launch traced here: 108 us
  Pallas kernels  101 us (93%)
  local copies, waits for them, and re-layouts  6.42 us (6%)
    pallas_call x1, Pallas kernels, by_kernel(): pl.pallas_call(functools.partial(fused, peers, cap), out_shape=(jax.Shape...  101 us
    unnamed x11, local copies, waits for them, and re-layouts  6.42 us

commit v1 on v0

--- a/solution.py
+++ b/solution.py
@@ -143,12 +143,12 @@
 
 def fused(
     peers, cap, tok_hbm, cot_hbm, wg_hbm, wu_hbm, wd_hbm, owner_ref, row_ref, gates_ref,
-    tg_out, gg_out, gu_out, gd_out, gr_out,
+    tg_out, own_a_out, x_got_a, own_b_out, x_got_b, gr_out,
     tt, cc, wgu, wd, code_ref, sel, put, take, send, got, back_send, back_got,
-    rows, pre, dpre, hid, outg,
-    core_send_a, core_got_a, own_a, x_send_a, x_got_a,
-    core_send_b, core_got_b, own_b, x_send_b, x_got_b,
-    load_sem, send_sem, recv_sem, bsend_sem, brecv_sem, csend_sem, crecv_sem, xsend_sem, xrecv_sem,
+    sel_t, tg, rows, pre, dpre, hid, outg,
+    core_send_a, core_got_a, own_a, x_send_a,
+    core_send_b, core_got_b, own_b, x_send_b,
+    load_sem, send_sem, recv_sem, bsend_sem, brecv_sem, csend_sem, crecv_sem, xsend_sem, xrecv_sem, store_sem,
 ):
     me = lax.axis_index("expert")
     dp = lax.axis_index("dp")
@@ -193,7 +193,7 @@
     level = jnp.where(line < cap, line, line - cap).astype(F32)
     first = line < cap
     spots = lax.broadcasted_iota(jnp.int32, (tokens_here, 1), 0)
-    for k in ORDER + (0,):
+    def choose(k):
         wanted = code_ref[pl.ds(partners[k], 1), :]
         at_level = (wanted == level).astype(F32).astype(BF16)
         at_row = (row_ref[pl.ds(partners[k], 1), :] == spots).astype(F32).astype(BF16)
@@ -203,14 +203,15 @@
             first, 0.0, chosen
         ).astype(BF16)
 
-    pl.semaphore_wait(barrier, peers - 1 + 2)
-
     copies = []
     forward = {}
     for which, table in ((0, tt), (1, cc)):
-        loads[2 * which].wait()
-        loads[2 * which + 1].wait()
         for k in ORDER + (0,):
+            if which == 0:
+                choose(k)
+            if k == ORDER[0]:
+                loads[2 * which].wait()
+                loads[2 * which + 1].wait()
             for piece in range(0, half, 512):
                 picked = dot(
                     sel[pl.ds(k * slab, slab), :], table[:, pl.ds(piece, 512)]
@@ -219,6 +220,8 @@
                     send[which, k, :, pl.ds(piece, 512)] = picked
                 else:
                     got[which, k, :, pl.ds(piece, 512)] = picked
+            if which == 0 and k == ORDER[0]:
+                pl.semaphore_wait(barrier, peers - 1 + 2)
             if k:
                 copy = pltpu.make_async_remote_copy(
                     src_ref=send.at[which, k],
@@ -243,6 +246,7 @@
         put[pl.ds(k * slab, slab), pl.ds(slots, slots)] = right.astype(BF16)
     for part in range(0, peers * slab, 128):
         take[:, pl.ds(part, 128)] = put[pl.ds(part, 128), :].astype(F32).T.astype(BF16)
+        sel_t[:, pl.ds(part, 128)] = sel[pl.ds(part, 128), :].astype(F32).T.astype(BF16)
     weight = jnp.broadcast_to(gates_ref[...], (128, slots)).T[:, :1]
     for number in (4, 5, 6):
         loads[number].wait()
@@ -257,28 +261,94 @@
             rows[which, :, pl.ds(piece, 256)] = picked[:slots]
             rows[which, :, pl.ds(half + piece, 256)] = picked[slots:]
 
+    planes = (1 - plane, plane)
+    core_copies = {}
+    x_copies = {}
+    stores = []
+
+    def part(n, j, core_of):
+        columns = pl.ds(pl.multiple_of((planes[j] * 2 + core_of) * shard, shard), shard)
+        if n == 0:
+            return contract_first(rows[0, :, columns], dpre[...])
+        return contract_first(hid[...], rows[1, :, columns])
+
+    sums = (
+        (core_send_a, core_got_a, own_a, x_send_a, x_got_a, own_a_out),
+        (core_send_b, core_got_b, own_b, x_send_b, x_got_b, own_b_out),
+    )
+
+    def to_core(n, j):
+        src, dst = sums[n][:2]
+        src[j] = part(n, j, 1 - core).astype(BF16)
+        copy = pltpu.make_async_remote_copy(
+            src_ref=src.at[j],
+            dst_ref=dst.at[j],
+            send_sem=csend_sem.at[j, n],
+            recv_sem=crecv_sem.at[j, n],
+            device_id=(sibling, me),
+            device_id_type=MESH,
+        )
+        copy.start()
+        copies.append(copy)
+        core_copies[j, n] = copy
+
+    def keep(n, j):
+        sums[n][2][j] = part(n, j, core)
+
+    def to_plane(n):
+        _, near, own, src, dst, _ = sums[n]
+        core_copies[0, n].wait_recv()
+        src[...] = (own[0] + near[0].astype(F32)).astype(BF16)
+        copy = pltpu.make_async_remote_copy(
+            src_ref=src,
+            dst_ref=dst,
+            send_sem=xsend_sem.at[n],
+            recv_sem=xrecv_sem.at[n],
+            device_id=(across, me),
+            device_id_type=MESH,
+        )
+        copy.start()
+        copies.append(copy)
+        x_copies[n] = copy
+
+    def store(src, dst):
+        copy = pltpu.make_async_copy(src, dst, store_sem.at[len(stores)])
+        copy.start()
+        stores.append(copy)
+
+    def finish(n):
+        _, near, own, _, _, out = sums[n]
+        core_copies[1, n].wait_recv()
+        own[1] = own[1] + near[1].astype(F32)
+        store(own.at[1], out)
+
     pick(0)
     pre[...] = dot(rows[0], wgu[...])
+    pre_gate = pre[:, :ff]
+    hid[...] = (pre_gate * jax.nn.sigmoid(pre_gate) * pre[:, ff:] * weight).astype(BF16)
+
     pick(1)
+    to_core(1, 0)
     raw = contract_last(rows[1], wd[...])
     pre_gate = pre[:, :ff]
     pre_up = pre[:, ff:]
     sigma = jax.nn.sigmoid(pre_gate)
     activated = pre_gate * sigma
-    hidden = activated * pre_up
-    gate_rows = jnp.sum(hidden * raw, axis=1, keepdims=True)
-    gr_out[...] = jnp.broadcast_to(gate_rows, (slots, 128)).T[:1]
-    hid[...] = (hidden * weight).astype(BF16)
     d_hidden = raw * weight
     dpre[:, :ff] = (d_hidden * pre_up * sigma * (1.0 + pre_gate * (1.0 - sigma))).astype(BF16)
     dpre[:, ff:] = (d_hidden * activated).astype(BF16)
+    gate_rows = jnp.sum(activated * pre_up * raw, axis=1, keepdims=True)
+    gr_out[...] = jnp.broadcast_to(gate_rows, (slots, 128)).T[:1]
+    keep(1, 0)
+    to_plane(1)
 
     for piece in range(0, half, 512):
         for side in range(2):
             grad = contract_last(dpre[...], wgu[pl.ds(side * half + piece, 512), :])
             outg[pl.ds(side * slots, slots), pl.ds(piece, 512)] = grad.astype(BF16)
     backward = {}
-    for k in ORDER + (0,):
+
+    def give_back(k):
         for piece in range(0, half, 512):
             placed = dot(
                 put[pl.ds(k * slab, slab), :], outg[:, pl.ds(piece, 512)]
@@ -300,74 +370,33 @@
             copies.append(copy)
             backward[k] = copy
 
-    def parts(owner):
-        columns = pl.ds(pl.multiple_of(owner * shard, shard), shard)
-        return (
-            contract_first(rows[0, :, columns], dpre[...]),
-            contract_first(hid[...], rows[1, :, columns]),
-        )
-
-    planes = (1 - plane, plane)
-    core_copies = {}
-    for j in range(2):
-        one, two = parts(planes[j] * 2 + (1 - core))
-        core_send_a[j] = one.astype(BF16)
-        core_send_b[j] = two.astype(BF16)
-        for n, (src, dst) in enumerate(((core_send_a, core_got_a), (core_send_b, core_got_b))):
-            copy = pltpu.make_async_remote_copy(
-                src_ref=src.at[j],
-                dst_ref=dst.at[j],
-                send_sem=csend_sem.at[j, n],
-                recv_sem=crecv_sem.at[j, n],
-                device_id=(sibling, me),
-                device_id_type=MESH,
-            )
-            copy.start()
-            copies.append(copy)
-            core_copies[j, n] = copy
-        one, two = parts(planes[j] * 2 + core)
-        own_a[j] = one
-        own_b[j] = two
-        if j == 0:
-            x_copies = []
-            for n, (own, near, src, dst) in enumerate((
-                (own_a, core_got_a, x_send_a, x_got_a),
-                (own_b, core_got_b, x_send_b, x_got_b),
-            )):
-                core_copies[0, n].wait_recv()
-                src[...] = (own[0] + near[0].astype(F32)).astype(BF16)
-                copy = pltpu.make_async_remote_copy(
-                    src_ref=src,
-                    dst_ref=dst,
-                    send_sem=xsend_sem.at[n],
-                    recv_sem=xrecv_sem.at[n],
-                    device_id=(across, me),
-                    device_id_type=MESH,
-                )
-                copy.start()
-                copies.append(copy)
-                x_copies.append(copy)
-    core_copies[1, 0].wait_recv()
-    own_a[1] = own_a[1] + core_got_a[1].astype(F32)
-    core_copies[1, 1].wait_recv()
-    own_b[1] = own_b[1] + core_got_b[1].astype(F32)
-
-    x_copies[0].wait_recv()
-    total = own_a[1] + x_got_a[...].astype(F32)
-    gg_out[...] = total[:, :ff]
-    gu_out[...] = total[:, ff:]
-    x_copies[1].wait_recv()
-    gd_out[...] = own_b[1] + x_got_b[...].astype(F32)
+    for k in ORDER[:4]:
+        give_back(k)
+    to_core(0, 0)
+    for k in ORDER[4:] + (0,):
+        give_back(k)
+    keep(0, 0)
+    to_plane(0)
+    for n in (1, 0):
+        to_core(n, 1)
+        keep(n, 1)
+    finish(1)
+    finish(0)
 
     for k in ORDER:
         backward[k].wait_recv()
     flat_back = back_got.reshape(peers * slab, half)
     for piece in range(0, half, 256):
-        summed = contract_first(sel[...], flat_back[:, pl.ds(piece, 256)]).astype(BF16)
-        tg_out[:, pl.ds(piece, 256)] = summed[:tokens_here]
-        tg_out[:, pl.ds(half + piece, 256)] = summed[tokens_here:]
+        summed = dot(sel_t[...], flat_back[:, pl.ds(piece, 256)]).astype(BF16)
+        tg[:, pl.ds(piece, 256)] = summed[:tokens_here]
+        tg[:, pl.ds(half + piece, 256)] = summed[tokens_here:]
+    store(tg, tg_out)
+    x_copies[1].wait_recv()
+    x_copies[0].wait_recv()
     for copy in copies:
         copy.wait_send()
+    for copy in stores:
+        copy.wait()
 
 
 def by_kernel(cap, tokens, cotangent, w_gate, w_up, w_down, route_owner, route_row, gates):
@@ -383,13 +412,14 @@
         functools.partial(fused, peers, cap),
         out_shape=(
             jax.ShapeDtypeStruct((tokens_here, width), BF16),
-            jax.ShapeDtypeStruct((shard, ff), F32),
-            jax.ShapeDtypeStruct((shard, ff), F32),
+            jax.ShapeDtypeStruct((shard, 2 * ff), F32),
+            jax.ShapeDtypeStruct((shard, 2 * ff), BF16),
             jax.ShapeDtypeStruct((ff, shard), F32),
+            jax.ShapeDtypeStruct((ff, shard), BF16),
             jax.ShapeDtypeStruct((1, slots), F32),
         ),
         in_specs=[hbm] * 5 + [vmem] * 3,
-        out_specs=(vmem,) * 5,
+        out_specs=(hbm,) * 5 + (vmem,),
         scratch_shapes=[
             pltpu.VMEM((2 * tokens_here, half), BF16),
             pltpu.VMEM((2 * tokens_here, half), BF16),
@@ -403,6 +433,8 @@
             pltpu.VMEM((2, peers, slab, half), BF16),
             pltpu.VMEM((peers, slab, half), BF16),
             pltpu.VMEM((peers, slab, half), BF16),
+            pltpu.VMEM((2 * tokens_here, peers * slab), BF16),
+            pltpu.VMEM((tokens_here, width), BF16),
             pltpu.VMEM((2, slots, width), BF16),
             pltpu.VMEM((slots, 2 * ff), F32),
             pltpu.VMEM((slots, 2 * ff), BF16),
@@ -412,11 +444,9 @@
             pltpu.VMEM((2, shard, 2 * ff), BF16),
             pltpu.VMEM((2, shard, 2 * ff), F32),
             pltpu.VMEM((shard, 2 * ff), BF16),
-            pltpu.VMEM((shard, 2 * ff), BF16),
             pltpu.VMEM((2, ff, shard), BF16),
             pltpu.VMEM((2, ff, shard), BF16),
             pltpu.VMEM((2, ff, shard), F32),
-            pltpu.VMEM((ff, shard), BF16),
             pltpu.VMEM((ff, shard), BF16),
             dma((7,)),
             dma((2, peers)),
@@ -427,6 +457,7 @@
             dma((2, 2)),
             dma((2,)),
             dma((2,)),
+            dma((3,)),
         ],
         compiler_params=pltpu.CompilerParams(
             collective_id=0, has_side_effects=True, vmem_limit_bytes=56 * 1024 * 1024
@@ -436,8 +467,14 @@
         tokens[0], cotangent[0], w_gate[0], w_up[0], w_down[0],
         route_owner[0], route_row[0], gates[0],
     )
-    token_grads, gate_sum, up_sum, down_sum, gate_rows = outs
-    return token_grads[None], gate_sum[None], up_sum[None], down_sum[None], gate_rows[None]
+    token_grads, own_a, got_a, own_b, got_b, gate_rows = outs
+    return (
+        token_grads[None],
+        (own_a[:, :ff] + got_a[:, :ff].astype(F32))[None],
+        (own_a[:, ff:] + got_a[:, ff:].astype(F32))[None],
+        (own_b + got_b.astype(F32))[None],
+        gate_rows[None],
+    )
 
 
 def on_device_any(tokens, cotangent, w_gate, w_up, w_down, route_owner, route_row, gates):

time: 109 us -> 104 us (0.954)
  local copies, waits for them, and re-layouts: 6.42 us -> 1.37 us
  other arithmetic: 0 us -> 4.84 us
  Pallas kernels: 101 us -> 96.8 us
    unnamed x11 -> x8, local copies, waits for them, and re-layouts: 6.42 us -> 1.37 us
    broadcast_in_dim x0 -> x2, other arithmetic: none -> 4.84 us  [the longest x1 2.5 us: by_kernel(): (own_a[:, ff:] + got_a[:, ff:].astype(F32))[None]]
    pallas_call x1, Pallas kernels: 101 us -> 96.8 us  [by_kernel(): pl.pallas_call(functools.partial(fused, peers, cap), out_shape=(jax.Shape...]
where the time goes in v1:
time: 104 us
  Pallas kernels  96.8 us (93%)
  other arithmetic  4.84 us (5%)
  local copies, waits for them, and re-layouts  1.37 us (1%)
    pallas_call x1, Pallas kernels, by_kernel(): pl.pallas_call(functools.partial(fused, peers, cap), out_shape=(jax.Shape...  96.8 us
    broadcast_in_dim x1, other arithmetic, by_kernel(): (own_a[:, ff:] + got_a[:, ff:].astype(F32))[None]  2.5 us
    broadcast_in_dim x1, other arithmetic, by_kernel(): (own_b + got_b.astype(F32))[None]  2.34 us

profile of v1, /device:TPU:1, one launch (start us, length us, event | category | flops | bytes accessed | tf_op | source)
XLA Modules:
  0.0 103.6 jit_solution(14326405779015818886)
XLA Ops:
  0.6 96.8 %moe_backward.1 = (bf16[128,2048]{1,0:T(8,128)(2,1)}, f32[512,768]{1,0:T(8,128)}, bf16[512,768]{1,0:T(8,128)(2,1)}, f32[384,512]{1,0:T(8,128)}, bf16[384,512]{1,0:T(8,128)(2,1)}, /*index=5*/f32[1,256]{1,0:T(1,128)}) custom-call(bf16[128,2048]{1,0:T(8,128)(2,1)} %bitcast.19, bf16[128,2048]{1,0:T(8,128)(2,1)} %bitcast.20, bf16[2048,384]{1,0:T(8,128)(2,1)} %bitcast.16, ...), custom_call_target="tpu_custom_call" | custom-call | tf_op jit(solution)/shard_map/moe_backward/pallas_call | solution.py:411
  97.4 0.0 copy-start
  97.4 2.3 %add_bitcast_fusion = f32[1,384,512]{2,1,0:T(8,128)} fusion(f32[384,512]{1,0:T(8,128)} %get-tuple-element.14, bf16[384,512]{1,0:T(8,128)(2,1)} %get-tuple-element.15), kind=kLoop, calls=%fused_computation | loop fusion | flops 393216 | bytes 1966080 | tf_op jit(solution)/shard_map/broadcast_in_dim | solution.py:475
  99.8 0.0 copy-done
  99.8 0.0 copy-start.1
  99.8 0.0 copy-start.2
  99.8 2.5 %add_bitcast_fusion.1 = (f32[1,512,384]{2,1,0:T(8,128)}, f32[1,512,384]{2,1,0:T(8,128)}) fusion(f32[512,768]{1,0:T(8,128)S(1)} %copy-done, bf16[512,768]{1,0:T(8,128)(2,1)} %get-tuple-element.13), kind=kLoop, calls=%fused_computation.1 | loop fusion | flops 786432 | bytes 3932160 | tf_op jit(solution)/shard_map/broadcast_in_dim | solution.py:474
  102.3 0.0 copy-done.1
  102.3 0.8 copy.15
  103.1 0.0 copy-done.2
  103.1 0.6 copy.16
Async XLA Ops:
  97.4 2.4 %copy-start = (f32[512,768]{1,0:T(8,128)S(1)}, f32[512,768]{1,0:T(8,128)}, u32[]{:S(2)}) copy-start(f32[512,768]{1,0:T(8,128)} %get-tuple-element.12) | copy-start | bytes 4718596
  99.8 2.5 %copy-start.1 = (bf16[128,2048]{1,0:T(8,128)(2,1)S(1)}, bf16[128,2048]{1,0:T(8,128)(2,1)}, u32[]{:S(2)}) copy-start(bf16[128,2048]{1,0:T(8,128)(2,1)} %get-tuple-element.11) | copy-start | bytes 1572868
  99.8 3.3 %copy-start.2 = (f32[1,256]{1,0:T(1,128)S(1)}, f32[1,256]{1,0:T(1,128)}, u32[]{:S(2)}) copy-start(f32[1,256]{1,0:T(1,128)} %get-tuple-element.16) | copy-start | bytes 3076
